TPU v7x, 256 devices: a whole 4x4x8 slice. The times are simulated.
256 devices in a mesh: dp: 16 (over y, x), ctx: 16 (over z, core).
Axes of the slice: x: 4, y: 4, z: 8, core: 2. Of those that a mesh axis runs over, the one named last changes fastest.
Arguments:
- queries: bfloat16 [65536, 512], P(('dp', 'ctx')), parts along dimension 0, may hold values from -32 to 32
- keys: bfloat16 [65536, 128], P(('dp', 'ctx')), parts along dimension 0, may hold values from -6 to 6
- values: bfloat16 [65536, 128], P(('dp', 'ctx')), parts along dimension 0, may hold values from -6 to 6
- out_grad: bfloat16 [65536, 512], P(('dp', 'ctx')), parts along dimension 0, may hold values from -6 to 6
- span_order: int32 [512], P('dp'), parts along dimension 0, may hold values from 0 to 31, each once
Outputs:
- query_grad: bfloat16 [65536, 512], P(('dp', 'ctx')), parts along dimension 0
- key_grad: bfloat16 [65536, 128], P(('dp', 'ctx')), parts along dimension 0
- value_grad: bfloat16 [65536, 128], P(('dp', 'ctx')), parts along dimension 0
There are 16 independent parts, one for each index of `dp`. A program takes and returns all parts, laid end to end along the dimension named above; each array names one. Nothing has to cross between parts.
All inputs are finite; a program needn't handle non-finite values.
Results may differ from a plain program's by a relative error of at most 0.02.
Values may be sent and summed in bfloat16 or wider, within the bound.
A program may use at most 128 MiB of HBM per device.

v0:
```python
import jax
import jax.numpy as jnp
from jax import lax
from jax.sharding import PartitionSpec as P


def head_scores(query_head, grad_head, block, block_pos, own_pos, softmax_scale):
    head_size = query_head.shape[1]
    key_block = block[:, :head_size]
    value_block = block[:, head_size:]
    scores = (
        jnp.einsum("id,jd->ij", query_head, key_block, preferred_element_type=jnp.float32)
        * softmax_scale
    )
    prob_grad = jnp.einsum("id,jd->ij", grad_head, value_block, preferred_element_type=jnp.float32)
    visible = block_pos[None, :] <= own_pos[:, None]
    return (scores, prob_grad, visible)


def on_device(queries, keys, values, out_grad, span_order):
    rows_here = queries.shape[0]
    head_size = keys.shape[1]
    head_count = queries.shape[1] // head_size
    half_rows = rows_here // 2
    softmax_scale = head_size ** (-0.5)
    all_pos = (
        span_order[:, None] * half_rows + jnp.arange(half_rows, dtype=jnp.int32)[None, :]
    ).reshape(-1)
    total_rows = all_pos.shape[0]
    own_index = lax.axis_index("ctx")
    own_pos = lax.dynamic_slice_in_dim(all_pos, own_index * rows_here, rows_here)
    stacked = jnp.concatenate([keys, values], axis=1)
    query_heads = [queries[:, h * head_size : (h + 1) * head_size] for h in range(head_count)]
    grad_heads = [out_grad[:, h * head_size : (h + 1) * head_size] for h in range(head_count)]
    term = None
    gathered = lax.all_gather(stacked, "ctx", axis=0, tiled=True)
    key_all = gathered[:, :head_size]
    term = jnp.zeros((total_rows, 2 * head_size), jnp.float32)
    query_parts = []
    log_list = []
    delta_list = []
    for h in range(head_count):
        scores, prob_grad, visible = head_scores(
            query_heads[h], grad_heads[h], gathered, all_pos, own_pos, softmax_scale
        )
        masked = jnp.where(visible, scores, -jnp.inf)
        row_max = jnp.max(masked, axis=1)
        log_head = row_max + jnp.log(jnp.sum(jnp.exp(masked - row_max[:, None]), axis=1))
        prob = jnp.where(visible, jnp.exp(scores - log_head[:, None]), 0.0)
        delta_head = jnp.sum(prob * prob_grad, axis=1)
        log_list.append(log_head)
        delta_list.append(delta_head)
        prob_low = prob.astype(jnp.bfloat16)
        score_grad = (prob * (prob_grad - delta_head[:, None]) * softmax_scale).astype(jnp.bfloat16)
        query_parts.append(
            jnp.dot(score_grad, key_all, preferred_element_type=jnp.float32).astype(jnp.bfloat16)
        )
        key_term = jnp.einsum(
            "ij,id->jd", score_grad, query_heads[h], preferred_element_type=jnp.float32
        )
        value_term = jnp.einsum(
            "ij,id->jd", prob_low, grad_heads[h], preferred_element_type=jnp.float32
        )
        term = term + jnp.concatenate([key_term, value_term], axis=1)
    query_grad = jnp.concatenate(query_parts, axis=1)
    summed = lax.psum_scatter(
        term.astype(jnp.bfloat16), "ctx", scatter_dimension=0, tiled=True
    ).astype(jnp.float32)
    key_grad = summed[:, :head_size].astype(jnp.bfloat16)
    value_grad = summed[:, head_size:].astype(jnp.bfloat16)
    return (query_grad, key_grad, value_grad)


def solution(mesh):
    placed = (
        P(("dp", "ctx"), None),
        P(("dp", "ctx"), None),
        P(("dp", "ctx"), None),
        P(("dp", "ctx"), None),
        P("dp"),
    )
    return jax.shard_map(
        on_device,
        mesh=mesh,
        in_specs=placed,
        out_specs=(P(("dp", "ctx"), None), P(("dp", "ctx"), None), P(("dp", "ctx"), None)),
        check_vma=False,
    )
```

profile of v0, /device:TPU:1, one launch (start us, length us, event | category | flops | bytes accessed | tf_op | source)
XLA Modules:
  0.0 171.7 jit_solution(9041428464620847374)
XLA Ops:
  7.2 1.6 pad_maximum_fusion.1
  8.9 0.7 broadcast_multiply_fusion
  9.7 44.7 %all-gather.2.cloned.1.call-done = bf16[4096,256]{1,0:T(8,128)(2,1)} async-done(((bf16[256,256]{1,0:T(8,128)(2,1)}), bf16[4096,256]{1,0:T(8,128)(2,1)}) %all-gather.2.cloned.1.call-update) | async-done | bytes 2097168 | tf_op jit(solution)/shard_map/all_gather | solution.py:36
  54.4 2.1 %fusion.1 = f32[256,4096]{0,1:T(8,128)S(1)} fusion(bf16[4096,256]{1,0:T(8,128)(2,1)} %all-gather.2.cloned.1.call-done, bf16[256,512]{1,0:T(8,128)(2,1)} %param.5), kind=kOutput, calls=%fused_computation.15 | convolution fusion | flops 269484032 | bytes 5308416 | tf_op jit(solution)/shard_map/id,jd->ij/dot_general | solution.py:12
  56.5 0.7 fusion.2
  57.2 0.9 fusion.7
  58.1 2.1 %exponential_reduce_fusion.3 = (f32[256]{0:T(256)S(1)}, f32[256]{0:T(256)S(1)}, f32[256]{0:T(256)S(1)}, f32[256]{0:T(256)S(1)}, f32[256,4096]{0,1:T(8,128)S(1)}) fusion(f32[256,4096]{0,1:T(8,128)S(1)} %get-tuple-element.24, f32[256]{0:T(256)S(1)} %get-tuple-element.23, s32[256]{0:T(256)S(1)} %dynamic_slice.3, s32[4096]{0:T(1024)S(1)} %add_bitcast_fusion, ...), kind=kOutput, calls=%fused_computation.35 | convolution fusion | flops 279968768 | bytes 17913856 | tf_op jit(solution)/shard_map/id,jd->ij/dot_general | solution.py:12
  60.3 2.7 %exponential_reduce_fusion.2 = (f32[256]{0:T(256)S(1)}, f32[256]{0:T(256)S(1)}, f32[256]{0:T(256)S(1)}) fusion(f32[256,4096]{0,1:T(8,128)S(1)} %fusion.2, f32[256]{0:T(256)S(1)} %get-tuple-element.13, s32[256]{0:T(256)S(1)} %dynamic_slice.3, s32[4096]{0:T(1024)S(1)} %add_bitcast_fusion, f32[256]{0:T(256)S(1)} %get-tuple-element.12, ...), kind=kLoop, calls=%fused_computation.32 | loop fusion | flops 10484992 | bytes 12606464 | tf_op jit(solution)/shard_map/reduce_sum | solution.py:48
  63.0 3.0 %fusion.15 = f32[4096,128]{0,1:T(8,128)} fusion(f32[256,4096]{0,1:T(8,128)S(1)} %get-tuple-element.25, f32[256]{0:T(256)S(1)} %get-tuple-element.27, s32[256]{0:T(256)S(1)} %dynamic_slice.3, s32[4096]{0:T(1024)S(1)} %add_bitcast_fusion, bf16[256,512]{1,0:T(8,128)(2,1)S(1)} %copy-done.12), kind=kOutput, calls=%fused_computation.44 | convolution fusion | flops 272629760 | bytes 6375424 | tf_op jit(solution)/shard_map/ij,id->jd/dot_general | solution.py:61
  66.0 2.9 %fusion.17 = f32[4096,128]{0,1:T(8,128)} fusion(f32[256,4096]{0,1:T(8,128)S(1)} %fusion.1, f32[256]{0:T(256)S(1)} %get-tuple-element.28, s32[256]{0:T(256)S(1)} %dynamic_slice.3, s32[4096]{0:T(1024)S(1)} %add_bitcast_fusion, bf16[256,512]{1,0:T(8,128)(2,1)S(1)} %copy-done.12), kind=kOutput, calls=%fused_computation.45 | convolution fusion | flops 272629760 | bytes 6375424 | tf_op jit(solution)/shard_map/ij,id->jd/dot_general | solution.py:61
  68.9 2.9 %fusion.21 = f32[4096,128]{0,1:T(8,128)} fusion(f32[256,4096]{0,1:T(8,128)S(1)} %get-tuple-element.24, f32[256]{0:T(256)S(1)} %get-tuple-element.30, s32[256]{0:T(256)S(1)} %dynamic_slice.3, s32[4096]{0:T(1024)S(1)} %add_bitcast_fusion, bf16[256,512]{1,0:T(8,128)(2,1)S(1)} %copy-done.12), kind=kOutput, calls=%fused_computation.47 | convolution fusion | flops 272629760 | bytes 6375424 | tf_op jit(solution)/shard_map/ij,id->jd/dot_general | solution.py:61
  71.8 2.9 %fusion.19 = f32[4096,128]{0,1:T(8,128)} fusion(f32[256,4096]{0,1:T(8,128)S(1)} %fusion.2, f32[256]{0:T(256)S(1)} %get-tuple-element.29, s32[256]{0:T(256)S(1)} %dynamic_slice.3, s32[4096]{0:T(1024)S(1)} %add_bitcast_fusion, bf16[256,512]{1,0:T(8,128)(2,1)S(1)} %copy-done.12), kind=kOutput, calls=%fused_computation.46 | convolution fusion | flops 272629760 | bytes 6375424 | tf_op jit(solution)/shard_map/ij,id->jd/dot_general | solution.py:61
  74.7 0.7 convolution_bitcast_fusion
  75.4 2.6 %convolution_bitcast_fusion.1 = f32[256,4096]{0,1:T(8,128)} fusion(bf16[4096,256]{1,0:T(8,128)(2,1)S(1)} %copy-done, bf16[256,512]{1,0:T(8,128)(2,1)S(1)} %copy-done.12), kind=kOutput, calls=%fused_computation.9 | convolution fusion | flops 268435456 | bytes 5308416 | tf_op jit(solution)/shard_map/id,jd->ij/dot_general | solution.py:15
  78.0 2.7 %convolution_bitcast_fusion.2 = f32[256,4096]{0,1:T(8,128)} fusion(bf16[4096,256]{1,0:T(8,128)(2,1)S(1)} %copy-done, bf16[256,512]{1,0:T(8,128)(2,1)S(1)} %copy-done.12), kind=kOutput, calls=%fused_computation.10 | convolution fusion | flops 268435456 | bytes 5308416 | tf_op jit(solution)/shard_map/id,jd->ij/dot_general | solution.py:15
  80.7 8.6 %multiply_reduce_fusion.3 = (f32[256]{0:T(256)S(1)}, f32[256]{0:T(256)}, f32[256]{0:T(256)}, f32[256]{0:T(256)}, f32[256,4096]{0,1:T(8,128)}) fusion(f32[256,4096]{0,1:T(8,128)S(1)} %get-tuple-element.24, f32[256]{0:T(256)S(1)} %get-tuple-element.30, s32[256]{0:T(256)S(1)} %dynamic_slice.3, s32[4096]{0:T(1024)S(1)} %add_bitcast_fusion, ...), kind=kOutput, calls=%fused_computation.34 | convolution fusion | flops 286260224 | bytes 34694144 | tf_op jit(solution)/shard_map/id,jd->ij/dot_general | solution.py:15
  89.4 9.6 %multiply_convert_fusion.3 = (bf16[256,4096]{0,1:T(8,128)(2,1)}, bf16[256,4096]{0,1:T(8,128)(2,1)}, bf16[256,4096]{0,1:T(8,128)(2,1)S(1)}, bf16[256,4096]{0,1:T(8,128)(2,1)S(1)}) fusion(f32[256,4096]{0,1:T(8,128)} %get-tuple-element.26, f32[256,4096]{0,1:T(8,128)S(1)} %get-tuple-element.24, f32[256]{0:T(256)S(1)} %get-tuple-element.6, ...), kind=kLoop, calls=%fused_computation.33 | loop fusion | flops 26214400 | bytes 41968640 | tf_op jit(solution)/shard_map/convert_element_type | solution.py:54
  99.0 0.8 fusion.53
  99.8 0.8 fusion.58
  101.1 1.0 copy-done.8
  102.1 0.8 fusion.63
  102.9 0.8 fusion.68
  103.8 0.6 copy-done.3
  104.4 0.6 copy-done.10
  105.7 2.4 %fusion.6 = bf16[4096,256]{0,1:T(8,128)(2,1)} fusion(f32[4096,128]{0,1:T(8,128)S(1)} %copy-done.10, f32[4096,128]{0,1:T(8,128)S(1)} %fusion.68, f32[4096,128]{0,1:T(8,128)S(1)} %copy-done.11, f32[4096,128]{0,1:T(8,128)S(1)} %fusion.63, f32[4096,128]{0,1:T(8,128)S(1)} %copy-done.3, f32[4096,128]{0,1:T(8,128)S(1)} %fusion.58, f32[4096,128]{0,1:T(8,128)S(1)} %copy-done.2, ...), kind=kLoop, calls=%fused_computation.23 | loop fusion | flops 8388608 | bytes 18874368 | tf_op jit(solution)/shard_map/convert_element_type | solution.py:67
  108.1 2.3 %convolution_convert_fusion.3 = bf16[256,128]{0,1:T(8,128)(2,1)S(1)} fusion(bf16[256,4096]{0,1:T(8,128)(2,1)} %get-tuple-element.19, bf16[4096,256]{1,0:T(8,128)(2,1)S(1)} %copy-done.1), kind=kOutput, calls=%fused_computation.67 | convolution fusion | flops 268468224 | bytes 3211264 | tf_op jit(solution)/shard_map/dot_general | solution.py:56
  110.4 2.3 %convolution_convert_fusion.2 = bf16[256,128]{0,1:T(8,128)(2,1)S(1)} fusion(bf16[256,4096]{0,1:T(8,128)(2,1)} %get-tuple-element.20, bf16[4096,256]{1,0:T(8,128)(2,1)S(1)} %copy-done.1), kind=kOutput, calls=%fused_computation.66 | convolution fusion | flops 268468224 | bytes 3211264 | tf_op jit(solution)/shard_map/dot_general | solution.py:56
  113.8 0.8 copy.8
  114.7 47.8 %reduce-scatter.2.cloned.1.call-done = bf16[256,256]{0,1:T(8,128)(2,1)} async-done(((bf16[4096,256]{0,1:T(8,128)(2,1)}), bf16[256,256]{0,1:T(8,128)(2,1)}) %reduce-scatter.2.cloned.1.call-update) | async-done | bytes 131088 | tf_op jit(solution)/shard_map/reduce_scatter | solution.py:66
  162.5 0.9 fusion.75
  163.3 0.7 copy.10
  164.1 0.7 copy.9
  (40 shorter events, 2.6 us)
Async XLA Ops:
  7.2 49.3 %copy-start.13 = (bf16[256,512]{1,0:T(8,128)(2,1)S(1)}, bf16[256,512]{1,0:T(8,128)(2,1)}, u32[]{:S(2)}) copy-start(bf16[256,512]{1,0:T(8,128)(2,1)} %param.5) | copy-start | bytes 786436
  7.2 47.2 %all-gather.2.cloned.1.call-start = ((), (), s32[]{:S(2)}) async-start(), calls=%async_computation.1 | async-start | bytes 2228224 | tf_op jit(solution)/shard_map/all_gather | solution.py:36
  8.8 153.6 %reduce-scatter.2.cloned.1.call-start = ((), (), s32[]{:S(2)}) async-start(), calls=%async_computation.2 | async-start | bytes 2228224 | tf_op jit(solution)/shard_map/reduce_scatter | solution.py:66
  54.4 2.1 %copy-start = (bf16[4096,256]{1,0:T(8,128)(2,1)S(1)}, bf16[4096,256]{1,0:T(8,128)(2,1)}, u32[]{:S(2)}) copy-start(bf16[4096,256]{1,0:T(8,128)(2,1)} %all-gather.2.cloned.1.call-done) | copy-start | bytes 6291460
  60.2 2.7 %copy-start.12 = (bf16[256,512]{1,0:T(8,128)(2,1)S(1)}, bf16[256,512]{1,0:T(8,128)(2,1)}, u32[]{:S(2)}) copy-start(bf16[256,512]{1,0:T(8,128)(2,1)} %param.8) | copy-start | bytes 786436
  89.4 9.6 %copy-start.14 = (bf16[256,512]{1,0:T(8,128)(2,1)S(1)}, bf16[256,512]{1,0:T(8,128)(2,1)}, u32[]{:S(2)}) copy-start(bf16[256,512]{1,0:T(8,128)(2,1)} %param.5) | copy-start | bytes 786436
  98.9 1.7 copy-start.4
  98.9 2.1 %copy-start.6 = (bf16[256,4096]{0,1:T(8,128)(2,1)}, bf16[256,4096]{0,1:T(8,128)(2,1)S(1)}, u32[]{:S(2)}) copy-start(bf16[256,4096]{0,1:T(8,128)(2,1)S(1)} %get-tuple-element.21) | copy-start | bytes 6291460
  99.0 3.1 %copy-start.8 = (bf16[256,4096]{0,1:T(8,128)(2,1)S(1)}, bf16[256,4096]{0,1:T(8,128)(2,1)}, u32[]{:S(2)}) copy-start(bf16[256,4096]{0,1:T(8,128)(2,1)} %get-tuple-element.20) | copy-start | bytes 6291460
  99.0 3.1 %copy-start.15 = (bf16[256,512]{1,0:T(8,128)(2,1)S(1)}, bf16[256,512]{1,0:T(8,128)(2,1)}, u32[]{:S(2)}) copy-start(bf16[256,512]{1,0:T(8,128)(2,1)} %param.5) | copy-start | bytes 786436
  99.8 3.1 %copy-start.9 = (bf16[256,4096]{0,1:T(8,128)(2,1)S(1)}, bf16[256,4096]{0,1:T(8,128)(2,1)}, u32[]{:S(2)}) copy-start(bf16[256,4096]{0,1:T(8,128)(2,1)} %get-tuple-element.19) | copy-start | bytes 6291460
  102.1 1.7 %copy-start.2 = (f32[4096,128]{0,1:T(8,128)S(1)}, f32[4096,128]{0,1:T(8,128)}, u32[]{:S(2)}) copy-start(f32[4096,128]{0,1:T(8,128)} %fusion.15) | copy-start | bytes 6291460
  102.1 2.4 %copy-start.3 = (f32[4096,128]{0,1:T(8,128)S(1)}, f32[4096,128]{0,1:T(8,128)}, u32[]{:S(2)}) copy-start(f32[4096,128]{0,1:T(8,128)} %fusion.17) | copy-start | bytes 6291460
  102.1 3.0 %copy-start.10 = (f32[4096,128]{0,1:T(8,128)S(1)}, f32[4096,128]{0,1:T(8,128)}, u32[]{:S(2)}) copy-start(f32[4096,128]{0,1:T(8,128)} %fusion.21) | copy-start | bytes 6291460
  102.1 3.6 %copy-start.11 = (f32[4096,128]{0,1:T(8,128)S(1)}, f32[4096,128]{0,1:T(8,128)}, u32[]{:S(2)}) copy-start(f32[4096,128]{0,1:T(8,128)} %fusion.19) | copy-start | bytes 6291460
  105.7 2.4 %copy-start.1 = (bf16[4096,256]{1,0:T(8,128)(2,1)S(1)}, bf16[4096,256]{1,0:T(8,128)(2,1)}, u32[]{:S(2)}) copy-start(bf16[4096,256]{1,0:T(8,128)(2,1)} %all-gather.2.cloned.1.call-done) | copy-start | bytes 6291460
  108.1 4.6 %copy-start.7 = (bf16[256,4096]{0,1:T(8,128)(2,1)S(1)}, bf16[256,4096]{0,1:T(8,128)(2,1)}, u32[]{:S(2)}) copy-start(bf16[256,4096]{0,1:T(8,128)(2,1)} %copy-done.6) | copy-start | bytes 6291460
  110.4 2.9 %copy-start.5 = (bf16[256,4096]{0,1:T(8,128)(2,1)S(1)}, bf16[256,4096]{0,1:T(8,128)(2,1)}, u32[]{:S(2)}) copy-start(bf16[256,4096]{0,1:T(8,128)(2,1)} %copy-done.4) | copy-start | bytes 6291460
Sparse Core Ops, SparseCore 0:
  10.4 43.9 all-gather.1
  108.2 54.2 reduce-scatter.1
where the time goes:
time: 174 us; the launch traced here: 172 us
  waiting for transfers between devices  92.5 us (53%)
  matrix products  41.1 us (24%)
  other arithmetic  17 us (10%)
  between operations  14.3 us (8%)
  local copies, waits for them, and re-layouts  6.66 us (4%)
    reduce_scatter x1, waiting for transfers between devices, on_device(): lax.psum_scatter(term.astype(jnp.bfloat16), 'ctx', scatter_dimension=0, t...  47.8 us
    all_gather x1, waiting for transfers between devices, on_device(): gathered = lax.all_gather(stacked, 'ctx', axis=0, tiled=True)  44.7 us
    dot_general x4, matrix products, head_scores(): jnp.einsum('id,jd->ij', grad_head, value_block, preferred_element_type=jn...  14.6 us
    dot_general x4, matrix products, on_device(): jnp.einsum('ij,id->jd', prob_low, grad_heads[h], preferred_element_type=j...  11.7 us
    convert_element_type x1, other arithmetic, on_device(): (prob * (prob_grad - delta_head[:, None]) * softmax_scale).astype(jnp.bfl...  9.59 us
    dot_general x4, matrix products, head_scores(): jnp.einsum('id,jd->ij', query_head, key_block, preferred_element_type=jnp...  5.8 us
    unnamed x35, local copies, waits for them, and re-layouts  5.71 us
    dot_general x4, matrix products, on_device(): jnp.dot(score_grad, key_all, preferred_element_type=jnp.float32)  5.69 us
  transfers between devices with their start and end apart: 2, of which 2 were waited for; matrix products, arithmetic and copies ran while one was open for 4% of the time, Pallas kernels for 0%

commit v1 on v0

v1 whole, which is shorter than its diff:
```python
import functools
import math

import jax
import jax.numpy as jnp
from jax import lax
from jax.experimental import pallas as pl
from jax.experimental.pallas import tpu as pltpu
from jax.sharding import PartitionSpec as P

MESH = pl.DeviceIdType.MESH
F32 = jnp.float32
BF16 = jnp.bfloat16
HIDDEN = -1e30
UP, DOWN = 0, 1
KEY, VALUE = 0, 1


def block_positions(order_ref, device, rows, half_rows, shape, dim):
    index = lax.broadcasted_iota(jnp.int32, shape, dim)
    blocks = rows // half_rows
    position = None
    for b in range(blocks):
        here = order_ref[device * blocks + b] * half_rows + (index - b * half_rows)
        position = here if position is None else jnp.where(index >= b * half_rows, here, position)
    return position


def kernel(
    chips, heads, unroll,
    q_in, k_in, v_in, g_in, order_ref,
    dq_out, dk_out, dv_out,
    q_raw, g_raw, q_rows, g_rows, q_cols, g_cols,
    k_all, v_all, k_cols, e_all, p_all, m_all, l_all, d_all,
    stat_out, stat_in, factor, delta, query_pos,
    term, dq_cols, dq_recv, ring_out, ring_in, dq_stage, dk_stage, dv_stage,
    local_sem, pair_send, pair_recv, gather_send, gather_recv, ring_send, ring_recv,
):
    rows, head_size = k_in.shape
    half_rows = chips * 2 * rows // order_ref.shape[0]
    tiles = 2 * heads
    far = chips // 2
    softmax_scale = head_size ** (-0.5)
    exponent_scale = softmax_scale * math.log2(math.e)

    me = lax.axis_index("ctx")
    chip, core = me // 2, me % 2
    partner = chip * 2 + (1 - core)

    def at_chip(offset):
        return lax.rem(chip + (offset + chips), chips) * 2 + core

    above, below = at_chip(1), at_chip(-1)

    barrier = pltpu.get_barrier_semaphore()
    for other in (above, below, partner):
        pl.semaphore_signal(barrier, inc=1, device_id={"ctx": other}, device_id_type=MESH)

    own = [
        pltpu.make_async_copy(src, dst, local_sem.at[i])
        for i, (src, dst) in enumerate(
            ((k_in, k_all.at[0]), (v_in, v_all.at[0]), (q_in, q_raw.at[0]), (g_in, g_raw.at[0]))
        )
    ]
    for copy in own:
        copy.start()

    def slot(way, distance):
        return (chips - distance) % chips if way == UP else distance

    def gather_copy(way, distance, part):
        source = (k_in, v_in)[part] if distance == 1 else (k_all, v_all)[part].at[slot(way, distance - 1)]
        return pltpu.make_async_remote_copy(
            src_ref=source,
            dst_ref=(k_all, v_all)[part].at[slot(way, distance)],
            send_sem=gather_send.at[way, distance - 1, part],
            recv_sem=gather_recv.at[way, distance - 1, part],
            device_id={"ctx": above if way == UP else below},
            device_id_type=MESH,
        )

    def travels(way, distance, part):
        return distance < far or (distance == far and (way == UP) == (part == KEY))

    def pair_copy(index, source, target):
        return pltpu.make_async_remote_copy(
            src_ref=source,
            dst_ref=target,
            send_sem=pair_send.at[index],
            recv_sem=pair_recv.at[index],
            device_id={"ctx": partner},
            device_id_type=MESH,
        )

    def ring_copy(way, distance, part):
        return pltpu.make_async_remote_copy(
            src_ref=ring_out.at[way, distance - 1, part],
            dst_ref=ring_in.at[way, distance - 1, part],
            send_sem=ring_send.at[way, distance - 1, part],
            recv_sem=ring_recv.at[way, distance - 1, part],
            device_id={"ctx": above if way == UP else below},
            device_id_type=MESH,
        )

    started = []

    def start(copy):
        copy.start()
        started.append(copy)

    pl.semaphore_wait(barrier, 3)

    for part in (KEY, VALUE):
        for way in (UP, DOWN):
            start(gather_copy(way, 1, part))
    pair_q = pair_copy(0, q_in, q_raw.at[1])
    pair_g = pair_copy(1, g_in, g_raw.at[1])
    start(pair_q)
    start(pair_g)

    def spread(half):
        for h in range(heads):
            columns = slice(h * head_size, (h + 1) * head_size)
            for raw, by_row, by_col in ((q_raw, q_rows, q_cols), (g_raw, g_rows, g_cols)):
                tile = raw[half, :, columns]
                by_row[half * heads + h] = tile
                by_col[half * heads + h] = tile.T
        query_pos[half] = block_positions(order_ref, me if half == 0 else partner, rows, half_rows, (8, rows), 1)

    def pass_one(where, device):
        k_cols[where] = k_all[where].T
        key_pos = block_positions(order_ref, device, rows, half_rows, (rows, rows), 0)

        def one(t):
            keys = k_all[where]
            scores = jnp.dot(keys, q_cols[t], preferred_element_type=F32)
            visible = key_pos <= query_pos[t // heads, 0:1, :]
            scores = jnp.where(visible, scores, HIDDEN)
            top = jnp.max(scores, axis=0, keepdims=True)
            e = jnp.exp2((scores - top) * exponent_scale)
            prob_grad = jnp.dot(v_all[where], g_cols[t], preferred_element_type=F32)
            e_all[where, t] = e
            p_all[where, t] = prob_grad
            m_all[t, where : where + 1, :] = top
            l_all[t, where : where + 1, :] = jnp.sum(e, axis=0, keepdims=True)
            d_all[t, where : where + 1, :] = jnp.sum(e * prob_grad, axis=0, keepdims=True)

        def body(i, carry):
            for u in range(unroll):
                one(i * unroll + u)
            return carry

        lax.fori_loop(0, tiles // unroll, body, 0)

    for copy in own:
        copy.wait()
    spread(0)
    pair_q.wait_recv()
    pair_g.wait_recv()
    spread(1)

    def relay(distance, part):
        for way in (UP, DOWN):
            if travels(way, distance, part):
                gather_copy(way, distance, part).wait_recv()
                if distance < far and travels(way, distance + 1, part):
                    start(gather_copy(way, distance + 1, part))

    relay(1, KEY)
    pass_one(0, me)
    relay(1, VALUE)
    for distance in range(1, far + 1):
        if distance > 1:
            relay(distance, KEY)
            relay(distance, VALUE)
        if distance < far:
            pass_one(slot(UP, distance), at_chip(-distance))
        pass_one(slot(DOWN, distance), at_chip(distance))

    stat_out[...] = jnp.zeros_like(stat_out)
    for t in range(tiles):
        top = jnp.max(m_all[t], axis=0, keepdims=True)
        weight = jnp.exp2((m_all[t] - top) * exponent_scale)
        stat_out[t, 0:1, :] = top
        stat_out[t, 1:2, :] = jnp.sum(l_all[t] * weight, axis=0, keepdims=True)
        stat_out[t, 2:3, :] = jnp.sum(d_all[t] * weight, axis=0, keepdims=True)
        factor[t] = weight
    stat_copies = []
    for i in range(2):
        copy = pair_copy(
            2 + i,
            stat_out.at[pl.ds(i * heads, heads)],
            stat_in.at[pl.ds((1 - i) * heads, heads)],
        )
        start(copy)
        stat_copies.append(copy)
    for copy in stat_copies:
        copy.wait_recv()
    for t in range(tiles):
        top_here, top_there = stat_out[t, 0:1, :], stat_in[t, 0:1, :]
        top = jnp.maximum(top_here, top_there)
        here = jnp.exp2((top_here - top) * exponent_scale)
        there = jnp.exp2((top_there - top) * exponent_scale)
        inverse = 1.0 / (stat_out[t, 1:2, :] * here + stat_in[t, 1:2, :] * there)
        delta[t] = jnp.broadcast_to(
            (stat_out[t, 2:3, :] * here + stat_in[t, 2:3, :] * there) * inverse, delta.shape[1:]
        )
        factor[t] = factor[t] * (here * inverse)

    dq_cols[...] = jnp.zeros_like(dq_cols)
    term[...] = jnp.zeros_like(term)

    def pass_two(where):
        def one(t):
            prob = e_all[where, t] * factor[t, where : where + 1, :]
            score_grad = (prob * (p_all[where, t] - delta[t, 0:1, :])).astype(BF16)
            term[where, VALUE] += jnp.dot(prob.astype(BF16), g_rows[t], preferred_element_type=F32)
            term[where, KEY] += jnp.dot(score_grad, q_rows[t], preferred_element_type=F32)
            dq_cols[t] += jnp.dot(k_cols[where], score_grad, preferred_element_type=F32)

        def body(i, carry):
            for u in range(unroll):
                one(i * unroll + u)
            return carry

        lax.fori_loop(0, tiles // unroll, body, 0)

    def own_term(where, part):
        value = term[where, part]
        return value * softmax_scale if part == KEY else value

    def ring_step(way, distance, part):
        if not travels(way, distance, part):
            return
        value = own_term(slot(1 - way, distance), part)
        if distance < far and travels(way, distance + 1, part):
            ring_copy(way, distance + 1, part).wait_recv()
            value = value + ring_in[way, distance, part].astype(F32)
        ring_out[way, distance - 1, part] = value.astype(BF16)
        start(ring_copy(way, distance, part))

    pass_two(far)
    ring_step(UP, far, KEY)
    ring_step(DOWN, far, VALUE)
    for distance in range(far - 1, 0, -1):
        for way in (UP, DOWN):
            pass_two(slot(1 - way, distance))
            if distance == far - 1:
                ring_step(way, distance, VALUE if way == UP else KEY)
        if distance == 1:
            pass_two(0)
            pair_dq = pair_copy(4, dq_cols.at[pl.ds(heads, heads)], dq_recv)
            start(pair_dq)
        if distance == far - 1:
            ring_step(UP, distance, KEY)
            ring_step(DOWN, distance, VALUE)
        else:
            for part in (KEY, VALUE):
                for way in (UP, DOWN):
                    ring_step(way, distance, part)

    pair_dq.wait_recv()
    for h in range(heads):
        total = (dq_cols[h] + dq_recv[h]) * softmax_scale
        dq_stage[:, h * head_size : (h + 1) * head_size] = total.T.astype(BF16)
    out = [pltpu.make_async_copy(dq_stage, dq_out, local_sem.at[4])]
    out[0].start()
    for part, stage, target in ((KEY, dk_stage, dk_out), (VALUE, dv_stage, dv_out)):
        value = own_term(0, part)
        for way in (UP, DOWN):
            ring_copy(way, 1, part).wait_recv()
            value = value + ring_in[way, 0, part].astype(F32)
        stage[...] = value.astype(BF16)
        copy = pltpu.make_async_copy(stage, target, local_sem.at[5 + part])
        copy.start()
        out.append(copy)
    for copy in started:
        copy.wait_send()
    for copy in out:
        copy.wait()


def solution(mesh):
    devices = mesh.shape["ctx"]
    chips = devices // 2
    far = chips // 2

    def on_device(queries, keys, values, out_grad, span_order):
        rows, head_size = keys.shape
        heads = queries.shape[1] // head_size
        tiles = 2 * heads
        any_spec = pl.BlockSpec(memory_space=pl.ANY)
        vmem = pltpu.VMEM
        elements = chips * tiles * rows * rows
        return pl.pallas_call(
            functools.partial(kernel, chips, heads, 2),
            name="ring_attention_backward",
            out_shape=(
                jax.ShapeDtypeStruct(queries.shape, BF16),
                jax.ShapeDtypeStruct(keys.shape, BF16),
                jax.ShapeDtypeStruct(values.shape, BF16),
            ),
            in_specs=[any_spec] * 4 + [pl.BlockSpec(memory_space=pltpu.SMEM)],
            out_specs=(any_spec,) * 3,
            scratch_shapes=[
                vmem((2, rows, heads * head_size), BF16),
                vmem((2, rows, heads * head_size), BF16),
                vmem((tiles, rows, head_size), BF16),
                vmem((tiles, rows, head_size), BF16),
                vmem((tiles, head_size, rows), BF16),
                vmem((tiles, head_size, rows), BF16),
                vmem((chips, rows, head_size), BF16),
                vmem((chips, rows, head_size), BF16),
                vmem((chips, head_size, rows), BF16),
                vmem((chips, tiles, rows, rows), F32),
                vmem((chips, tiles, rows, rows), F32),
                vmem((tiles, chips, rows), F32),
                vmem((tiles, chips, rows), F32),
                vmem((tiles, chips, rows), F32),
                vmem((tiles, 8, rows), F32),
                vmem((tiles, 8, rows), F32),
                vmem((tiles, chips, rows), F32),
                vmem((tiles, 8, rows), F32),
                vmem((2, 8, rows), jnp.int32),
                vmem((chips, 2, rows, head_size), F32),
                vmem((tiles, head_size, rows), F32),
                vmem((heads, head_size, rows), F32),
                vmem((2, far, 2, rows, head_size), BF16),
                vmem((2, far, 2, rows, head_size), BF16),
                vmem((rows, heads * head_size), BF16),
                vmem((rows, head_size), BF16),
                vmem((rows, head_size), BF16),
                pltpu.SemaphoreType.DMA((7,)),
                pltpu.SemaphoreType.DMA((5,)),
                pltpu.SemaphoreType.DMA((5,)),
                pltpu.SemaphoreType.DMA((2, far, 2)),
                pltpu.SemaphoreType.DMA((2, far, 2)),
                pltpu.SemaphoreType.DMA((2, far, 2)),
                pltpu.SemaphoreType.DMA((2, far, 2)),
            ],
            compiler_params=pltpu.CompilerParams(
                collective_id=0,
                has_side_effects=True,
                vmem_limit_bytes=58 * 1024 * 1024,
            ),
            cost_estimate=pl.CostEstimate(
                flops=10 * elements * head_size,
                bytes_accessed=2 * (2 * queries.size * 2 + 3 * keys.size * 2),
                transcendentals=elements,
            ),
        )(queries, keys, values, out_grad, span_order)

    row = P(("dp", "ctx"), None)
    return jax.shard_map(
        on_device,
        mesh=mesh,
        in_specs=(row, row, row, row, P("dp")),
        out_specs=(row, row, row),
        check_vma=False,
    )
```

time: 174 us -> 51.9 us (0.30); the launches traced: 172 us -> 51.8 us
  waiting for transfers between devices: 92.5 us -> 0 us
  Pallas kernels: 0 us -> 47.9 us
  matrix products: 41.1 us -> 0 us
  other arithmetic: 17 us -> 0 us
  between operations: 14.3 us -> 0.65 us
  local copies, waits for them, and re-layouts: 6.66 us -> 3.2 us
    pallas_call x0 -> x1, Pallas kernels: none -> 47.9 us  [on_device(): pl.pallas_call(functools.partial(kernel, chips, heads, 2), name='ring_att...]
    reduce_scatter x1 -> x0, waiting for transfers between devices: 47.8 us -> none  [on_device(): lax.psum_scatter(term.astype(jnp.bfloat16), 'ctx', scatter_dimension=0, t...]
    all_gather x1 -> x0, waiting for transfers between devices: 44.7 us -> none  [on_device(): gathered = lax.all_gather(stacked, 'ctx', axis=0, tiled=True)]
    dot_general x20 -> x0, matrix products: 41.1 us -> none  [the longest x4 14.6 us: head_scores(): jnp.einsum('id,jd->ij', grad_head, value_block, preferred_element_type=jn...]
    convert_element_type x2 -> x0, other arithmetic: 12 us -> none  [the longest x1 9.59 us: on_device(): (prob * (prob_grad - delta_head[:, None]) * softmax_scale).astype(jnp.bfl...]
    reduce_sum x1 -> x0, other arithmetic: 2.71 us -> none  [on_device(): jnp.sum(jnp.exp(masked - row_max[:, None]), axis=1)]
    unnamed x35 -> x7, local copies, waits for them, and re-layouts: 5.71 us -> 3.2 us
  transfers between devices with their start and end apart: 2 -> 0, of which waited for: 2 -> 0; matrix products, arithmetic and copies ran while one was open for 4% -> 0% of each run, Pallas kernels for 0% -> 0%
where the time goes in v1:
time: 51.9 us; the launch traced here: 51.8 us
  Pallas kernels  47.9 us (92%)
  local copies, waits for them, and re-layouts  3.2 us (6%)
  between operations  0.65 us (1%)
    pallas_call x1, Pallas kernels, on_device(): pl.pallas_call(functools.partial(kernel, chips, heads, 2), name='ring_att...  47.9 us
    unnamed x7, local copies, waits for them, and re-layouts  3.2 us

profile of v1, /device:TPU:1, one launch (start us, length us, event | category | flops | bytes accessed | tf_op | source)
XLA Modules:
  0.0 51.8 jit_solution(13042955872585456824)
XLA Ops:
  0.6 47.9 %ring_attention_backward.1 = (bf16[256,512]{1,0:T(8,128)(2,1)}, bf16[256,128]{1,0:T(8,128)(2,1)}, bf16[256,128]{1,0:T(8,128)(2,1)}) custom-call(bf16[256,512]{1,0:T(8,128)(2,1)} %q_in.1, bf16[256,128]{1,0:T(8,128)(2,1)} %k_in.1, bf16[256,128]{1,0:T(8,128)(2,1)} %v_in.1, bf16[256,512]{1,0:T(8,128)(2,1)} %g_in.1, s32[32]{0:T(128)} %order_ref.1), custom_call_target="tpu_custom_call" | custom-call | flops 5368709120 | bytes 1441792 | tf_op jit(solution)/shard_map/ring_attention_backward/pallas_call | solution.py:295
  48.6 0.0 copy-start.1
  48.6 1.7 %copy.11 = bf16[256,512]{1,0:T(8,128)(2,1)} copy(bf16[256,512]{1,0:T(8,128)(2,1)} %get-tuple-element.6) | data formatting | bytes 524288
  50.3 0.0 copy-done.1
  50.3 0.0 copy-start
  50.3 0.6 %copy.12 = bf16[256,128]{1,0:T(8,128)(2,1)} copy(bf16[256,128]{1,0:T(8,128)(2,1)S(1)} %copy-done.1) | data formatting | bytes 131072
  50.9 0.2 copy-done
  51.1 0.6 %copy.13 = bf16[256,128]{1,0:T(8,128)(2,1)} copy(bf16[256,128]{1,0:T(8,128)(2,1)S(1)} %copy-done) | data formatting | bytes 131072
Async XLA Ops:
  48.6 1.7 %copy-start.1 = (bf16[256,128]{1,0:T(8,128)(2,1)S(1)}, bf16[256,128]{1,0:T(8,128)(2,1)}, u32[]{:S(2)}) copy-start(bf16[256,128]{1,0:T(8,128)(2,1)} %get-tuple-element.7) | copy-start | bytes 196612
  50.3 0.9 %copy-start = (bf16[256,128]{1,0:T(8,128)(2,1)S(1)}, bf16[256,128]{1,0:T(8,128)(2,1)}, u32[]{:S(2)}) copy-start(bf16[256,128]{1,0:T(8,128)(2,1)} %get-tuple-element.8) | copy-start | bytes 196612

commit v2 on v1

v2 whole, which is shorter than its diff:
```python
import functools
import math

import jax
import jax.numpy as jnp
from jax import lax
from jax.experimental import pallas as pl
from jax.experimental.pallas import tpu as pltpu
from jax.sharding import PartitionSpec as P

MESH = pl.DeviceIdType.MESH
F32 = jnp.float32
BF16 = jnp.bfloat16
HIDDEN = -1e30
UP, DOWN = 0, 1
KEY, VALUE = 0, 1


def block_of_row(order_ref, device, blocks, half_rows, shape):
    index = lax.broadcasted_iota(jnp.int32, shape, len(shape) - 1)
    result = jnp.full(shape, order_ref[device * blocks], jnp.int32)
    for b in range(1, blocks):
        result = jnp.where(index >= b * half_rows, order_ref[device * blocks + b], result)
    return result


def kernel(
    chips, heads,
    q_in, k_in, v_in, g_in, order_in,
    dq_out, dk_out, dv_out,
    q_raw, g_raw, q_cols, g_cols,
    k_all, v_all, k_cols, e_all, p_all, m_all, l_all, d_all,
    stat_out, stat_in, factor, delta, query_block, key_block,
    term, dq_cols, dq_recv, ring_out, ring_in, dq_stage, dk_stage, dv_stage,
    order_ref, local_sem, pair_send, pair_recv, sent, gather_recv, ring_recv,
):
    rows, head_size = k_in.shape
    half_rows = chips * 2 * rows // order_in.shape[0]
    blocks = rows // half_rows
    tiles = 2 * heads
    far = chips // 2
    softmax_scale = head_size ** (-0.5)
    exponent_scale = softmax_scale * math.log2(math.e)

    me = lax.axis_index("ctx")
    chip, core = me // 2, me % 2
    partner = chip * 2 + (1 - core)

    def at_chip(offset):
        return lax.rem(chip + (offset + chips), chips) * 2 + core

    above, below = at_chip(1), at_chip(-1)

    barrier = pltpu.get_barrier_semaphore()
    for other in (above, below, partner):
        pl.semaphore_signal(barrier, inc=1, device_id={"ctx": other}, device_id_type=MESH)

    own = [
        pltpu.make_async_copy(src, dst, local_sem.at[i])
        for i, (src, dst) in enumerate(
            ((q_in, q_raw.at[0]), (g_in, g_raw.at[0]), (k_in, k_all.at[0]), (v_in, v_all.at[0]), (order_in, order_ref))
        )
    ]
    for copy in own:
        copy.start()

    def slot(way, distance):
        return (chips - distance) % chips if way == UP else distance

    def head_columns(h):
        return slice(h * head_size, (h + 1) * head_size)

    def part_rows(b):
        return slice(b * half_rows, (b + 1) * half_rows)

    def gather_copy(way, distance, part, b):
        here = pl.ds(b * half_rows, half_rows)
        all_rows = (k_all, v_all)[part]
        return pltpu.make_async_remote_copy(
            src_ref=(k_in, v_in)[part].at[here] if distance == 1 else all_rows.at[slot(way, distance - 1), here],
            dst_ref=all_rows.at[slot(way, distance), here],
            send_sem=sent.at[0],
            recv_sem=gather_recv.at[way, distance - 1, part, b],
            device_id={"ctx": above if way == UP else below},
            device_id_type=MESH,
        )

    def travels(way, distance, b):
        return distance < far or (distance == far and (way == UP) == (b < blocks // 2))

    def pair_copy(index, source, target):
        return pltpu.make_async_remote_copy(
            src_ref=source,
            dst_ref=target,
            send_sem=pair_send.at[index],
            recv_sem=pair_recv.at[index],
            device_id={"ctx": partner},
            device_id_type=MESH,
        )

    def ring_copy(way, distance, part, b):
        return pltpu.make_async_remote_copy(
            src_ref=ring_out.at[way, distance - 1, part, b],
            dst_ref=ring_in.at[way, distance - 1, part, b],
            send_sem=sent.at[0],
            recv_sem=ring_recv.at[way, distance - 1, part, b],
            device_id={"ctx": above if way == UP else below},
            device_id_type=MESH,
        )

    started = []
    sends = []

    def start(copy, sends=started):
        copy.start()
        sends.append(copy)

    pl.semaphore_wait(barrier, 3)

    for part in (KEY, VALUE):
        for b in range(blocks):
            for way in (UP, DOWN):
                if travels(way, 1, b):
                    start(gather_copy(way, 1, part, b), sends)
    pair_q = pair_copy(0, q_in, q_raw.at[1])
    pair_g = pair_copy(1, g_in, g_raw.at[1])
    start(pair_q)
    start(pair_g)
    dq_cols[...] = jnp.zeros_like(dq_cols)
    stat_out[...] = jnp.zeros_like(stat_out)

    def spread(half):
        for h in range(heads):
            columns = head_columns(h)
            q_cols[half * heads + h] = q_raw[half, :, columns].T
            g_cols[half * heads + h] = g_raw[half, :, columns].T
        query_block[half] = block_of_row(order_ref, me if half == 0 else partner, blocks, half_rows, (8, rows))

    once = (me + 2 * chips) // (2 * chips)

    def over_tiles(body):
        def step(i, carry):
            body(range(tiles))
            return carry

        lax.fori_loop(0, once, step, 0)

    def pass_one(where, device, diagonal=False):
        k_cols[where] = k_all[where].T
        for b in range(blocks):
            key_block[where * blocks + b : where * blocks + b + 1, :] = jnp.full(
                (1, rows), order_ref[device * blocks + b], jnp.int32
            )

        def one(t):
            scores = jnp.dot(k_all[where], q_cols[t], preferred_element_type=F32)
            prob_grad = jnp.dot(v_all[where], g_cols[t], preferred_element_type=F32)
            p_all[where, t] = prob_grad
            for b in range(blocks):
                r = where * blocks + b
                block = scores[part_rows(b)]
                if diagonal and t < heads:
                    key_row = lax.broadcasted_iota(jnp.int32, block.shape, 0) + b * half_rows
                    query_row = lax.broadcasted_iota(jnp.int32, block.shape, 1)
                    limit = jnp.where(query_row < (b + 1) * half_rows, query_row, rows)
                    limit = jnp.where(query_row < b * half_rows, rows, limit)
                    block = jnp.where(key_row > limit, HIDDEN, block)
                top = jnp.max(block, axis=0, keepdims=True)
                e = jnp.exp2((block - top) * exponent_scale)
                e_all[where, t, part_rows(b)] = e
                m_all[t, r : r + 1, :] = top
                l_all[t, r : r + 1, :] = jnp.sum(e, axis=0, keepdims=True)
                d_all[t, r : r + 1, :] = jnp.sum(e * prob_grad[part_rows(b)], axis=0, keepdims=True)

        over_tiles(lambda group: [one(t) for t in group])

    def pass_two(where):
        def several(group):
            key_sum = value_sum = None
            for t in group:
                probs, score_grads = [], []
                for b in range(blocks):
                    r = where * blocks + b
                    prob = e_all[where, t, part_rows(b)] * factor[t, r : r + 1, :]
                    probs.append(prob.astype(BF16))
                    score_grads.append((prob * (p_all[where, t, part_rows(b)] - delta[t, 0:1, :])).astype(BF16))
                prob = jnp.concatenate(probs, axis=0)
                score_grad = jnp.concatenate(score_grads, axis=0)
                half, columns = t // heads, head_columns(t % heads)
                v = jnp.dot(prob, g_raw[half, :, columns], preferred_element_type=F32)
                k = jnp.dot(score_grad, q_raw[half, :, columns], preferred_element_type=F32)
                value_sum = v if value_sum is None else value_sum + v
                key_sum = k if key_sum is None else key_sum + k
                dq_cols[t] += jnp.dot(k_cols[where], score_grad, preferred_element_type=F32)
            term[where, VALUE] = value_sum
            term[where, KEY] = key_sum * softmax_scale

        over_tiles(several)

    for copy in own:
        copy.wait()
    spread(0)
    pair_q.wait_recv()
    pair_g.wait_recv()
    spread(1)

    def relay(distance, part):
        for b in range(blocks):
            for way in (UP, DOWN):
                if travels(way, distance, b):
                    gather_copy(way, distance, part, b).wait_recv()
                    if travels(way, distance + 1, b):
                        start(gather_copy(way, distance + 1, part, b), sends)

    work = [functools.partial(pass_one, 0, me, diagonal=True)]
    for distance in range(1, far):
        relay(distance, KEY)
        work.pop(0)()
        work.append(functools.partial(pass_one, slot(UP, distance), at_chip(-distance)))
        work.append(functools.partial(pass_one, slot(DOWN, distance), at_chip(distance)))
        relay(distance, VALUE)
        work.pop(0)()
    for item in work:
        item()
    relay(far, KEY)
    relay(far, VALUE)
    pass_one(far, at_chip(far))

    for t in range(tiles):
        visible = key_block[...] <= query_block[t // heads, 0:1, :]
        top = jnp.max(jnp.where(visible, m_all[t], HIDDEN), axis=0, keepdims=True)
        weight = jnp.where(visible, jnp.exp2((m_all[t] - top) * exponent_scale), 0.0)
        stat_out[t, 0:1, :] = top
        stat_out[t, 1:2, :] = jnp.sum(l_all[t] * weight, axis=0, keepdims=True)
        stat_out[t, 2:3, :] = jnp.sum(d_all[t] * weight, axis=0, keepdims=True)
        factor[t] = weight
    stat_copies = []
    for i in range(2):
        here, there = pl.ds(i * heads, heads), pl.ds((1 - i) * heads, heads)
        stat_copies.append(pair_copy(2 + i, stat_out.at[here], stat_in.at[there]))
        start(stat_copies[-1])
    for copy in stat_copies:
        copy.wait_recv()
    for t in range(tiles):
        top_here, top_there = stat_out[t, 0:1, :], stat_in[t, 0:1, :]
        top = jnp.maximum(top_here, top_there)
        here = jnp.exp2((top_here - top) * exponent_scale)
        there = jnp.exp2((top_there - top) * exponent_scale)
        inverse = 1.0 / (stat_out[t, 1:2, :] * here + stat_in[t, 1:2, :] * there)
        delta[t, 0:1, :] = (stat_out[t, 2:3, :] * here + stat_in[t, 2:3, :] * there) * inverse
        factor[t] = factor[t] * (here * inverse)

    def ring_step(way, distance, part, b):
        if not travels(way, distance, b):
            return
        value = term[slot(1 - way, distance), part, part_rows(b)]
        if travels(way, distance + 1, b):
            ring_copy(way, distance + 1, part, b).wait_recv()
            value = value + ring_in[way, distance, part, b].astype(F32)
        ring_out[way, distance - 1, part, b] = value.astype(BF16)
        start(ring_copy(way, distance, part, b), sends)

    def ring_steps(distance, part, first):
        for way in (UP, DOWN):
            for b in range(blocks):
                if travels(way, far, b) != first:
                    ring_step(way, distance, part, b)

    near = far - 1
    pass_two(far)
    for part in (KEY, VALUE):
        ring_steps(far, part, False)
    work = []
    for distance in range(near, 0, -1):
        for way in (UP, DOWN):
            work.append((distance, way))
    for distance, way in work[:2]:
        pass_two(slot(1 - way, distance))
        for part in (KEY, VALUE):
            for b in range(blocks):
                if not travels(way, far, b):
                    ring_step(way, distance, part, b)
    work = [functools.partial(pass_two, slot(1 - way, distance)) for distance, way in work[2:]]
    work.append(functools.partial(pass_two, 0))
    work.pop(0)()
    ring_steps(near, KEY, False)
    ring_steps(near, VALUE, False)
    for distance in range(near - 1, 0, -1):
        work.pop(0)()
        ring_steps(distance, KEY, True)
        ring_steps(distance, VALUE, True)
        if work:
            work.pop(0)()
        if distance == 1:
            for item in work:
                item()
            pair_dq = pair_copy(4, dq_cols.at[pl.ds(heads, heads)], dq_recv)
            start(pair_dq)
        ring_steps(distance, KEY, False)
        ring_steps(distance, VALUE, False)

    pair_dq.wait_recv()
    for h in range(heads):
        total = (dq_cols[h] + dq_recv[h]) * softmax_scale
        dq_stage[:, head_columns(h)] = total.T.astype(BF16)
    out = [pltpu.make_async_copy(dq_stage, dq_out, local_sem.at[5])]
    out[0].start()
    for part, stage, target in ((VALUE, dv_stage, dv_out), (KEY, dk_stage, dk_out)):
        for b in range(blocks):
            value = term[0, part, part_rows(b)]
            for way in (UP, DOWN):
                ring_copy(way, 1, part, b).wait_recv()
                value = value + ring_in[way, 0, part, b].astype(F32)
            stage[part_rows(b)] = value.astype(BF16)
        copy = pltpu.make_async_copy(stage, target, local_sem.at[6 + part])
        copy.start()
        out.append(copy)
    tile_sends = 2 * rows // half_rows * rows // head_size
    assert len(sends) % tile_sends == 0
    span = e_all.at[0, pl.ds(0, len(sends) // tile_sends)]
    pltpu.make_async_copy(span, span, sent.at[0]).wait()
    for copy in started:
        copy.wait_send()
    for copy in out:
        copy.wait()


def hand_over(*refs):
    count = len(refs) // 2
    for source, target in zip(refs[:count], refs[count:]):
        target[...] = source[...]


def solution(mesh):
    devices = mesh.shape["ctx"]
    chips = devices // 2
    far = chips // 2

    def on_device(queries, keys, values, out_grad, span_order):
        rows, head_size = keys.shape
        heads = queries.shape[1] // head_size
        tiles = 2 * heads
        spans = span_order.shape[0] // 2
        half_rows = devices * rows // span_order.shape[0]
        blocks = rows // half_rows
        any_spec = pl.BlockSpec(memory_space=pl.ANY)
        hbm_spec = pl.BlockSpec(memory_space=pltpu.HBM)
        vmem = pltpu.VMEM
        elements = chips * tiles * rows * rows
        out_shape = (
            jax.ShapeDtypeStruct(queries.shape, BF16),
            jax.ShapeDtypeStruct(keys.shape, BF16),
            jax.ShapeDtypeStruct(values.shape, BF16),
        )
        ring_semaphores = pltpu.SemaphoreType.DMA((2, far, 2, blocks))
        results = pl.pallas_call(
            functools.partial(kernel, chips, heads),
            name="ring_attention_backward",
            out_shape=out_shape,
            in_specs=[hbm_spec] * 5,
            out_specs=(any_spec,) * 3,
            scratch_shapes=[
                vmem((2, rows, heads * head_size), BF16),
                vmem((2, rows, heads * head_size), BF16),
                vmem((tiles, head_size, rows), BF16),
                vmem((tiles, head_size, rows), BF16),
                vmem((chips, rows, head_size), BF16),
                vmem((chips, rows, head_size), BF16),
                vmem((chips, head_size, rows), BF16),
                vmem((chips, tiles, rows, rows), F32),
                vmem((chips, tiles, rows, rows), F32),
                vmem((tiles, spans, rows), F32),
                vmem((tiles, spans, rows), F32),
                vmem((tiles, spans, rows), F32),
                vmem((tiles, 8, rows), F32),
                vmem((tiles, 8, rows), F32),
                vmem((tiles, spans, rows), F32),
                vmem((tiles, 8, rows), F32),
                vmem((2, 8, rows), jnp.int32),
                vmem((spans, rows), jnp.int32),
                vmem((chips, 2, rows, head_size), F32),
                vmem((tiles, head_size, rows), F32),
                vmem((heads, head_size, rows), F32),
                vmem((2, far, 2, blocks, half_rows, head_size), BF16),
                vmem((2, far, 2, blocks, half_rows, head_size), BF16),
                vmem((rows, heads * head_size), BF16),
                vmem((rows, head_size), BF16),
                vmem((rows, head_size), BF16),
                pltpu.SMEM(span_order.shape, jnp.int32),
                pltpu.SemaphoreType.DMA((8,)),
                pltpu.SemaphoreType.DMA((5,)),
                pltpu.SemaphoreType.DMA((5,)),
                pltpu.SemaphoreType.DMA((1,)),
                ring_semaphores,
                ring_semaphores,
            ],
            compiler_params=pltpu.CompilerParams(
                collective_id=0,
                has_side_effects=True,
                vmem_limit_bytes=58 * 1024 * 1024,
            ),
            cost_estimate=pl.CostEstimate(
                flops=10 * elements * head_size,
                bytes_accessed=2 * (2 * queries.size * 2 + 3 * keys.size * 2),
                transcendentals=elements,
            ),
        )(queries, keys, values, out_grad, span_order)
        return pl.pallas_call(
            hand_over,
            name="hand_over",
            out_shape=out_shape,
            in_specs=[pl.BlockSpec(memory_space=pltpu.VMEM)] * 3,
            out_specs=(pl.BlockSpec(memory_space=pltpu.VMEM),) * 3,
        )(*results)

    row = P(("dp", "ctx"), None)
    return jax.shard_map(
        on_device,
        mesh=mesh,
        in_specs=(row, row, row, row, P("dp")),
        out_specs=(row, row, row),
        check_vma=False,
    )
```

time: 51.9 us -> 43.6 us (0.84)
  Pallas kernels: 47.9 us -> 42.8 us
  local copies, waits for them, and re-layouts: 3.2 us -> 0 us
    pallas_call x1 -> x2, Pallas kernels: 47.9 us -> 42.8 us  [the longest x1 41.1 us: on_device(): pl.pallas_call(functools.partial(kernel, chips, heads), name='ring_attent...]
    unnamed x7 -> x0, local copies, waits for them, and re-layouts: 3.2 us -> none
where the time goes in v2:
time: 43.6 us; the launch traced here: 43.5 us
  Pallas kernels  42.8 us (98%)
  between operations  0.64 us (1%)
    pallas_call x1, Pallas kernels, on_device(): pl.pallas_call(functools.partial(kernel, chips, heads), name='ring_attent...  41.1 us
    pallas_call x1, Pallas kernels, on_device(): pl.pallas_call(hand_over, name='hand_over', out_shape=out_shape, in_specs...  1.73 us

profile of v2, /device:TPU:1, one launch (start us, length us, event | category | flops | bytes accessed | tf_op | source)
XLA Modules:
  0.0 43.5 jit_solution(8722227025144368835)
XLA Ops:
  0.6 41.1 %ring_attention_backward.1 = (bf16[256,512]{1,0:T(8,128)(2,1)}, bf16[256,128]{1,0:T(8,128)(2,1)}, bf16[256,128]{1,0:T(8,128)(2,1)}) custom-call(bf16[256,512]{1,0:T(8,128)(2,1)} %q_in.1, bf16[256,128]{1,0:T(8,128)(2,1)} %k_in.1, bf16[256,128]{1,0:T(8,128)(2,1)} %v_in.1, bf16[256,512]{1,0:T(8,128)(2,1)} %g_in.1, s32[32]{0:T(128)} %order_in.1), custom_call_target="tpu_custom_call" | custom-call | flops 5368709120 | bytes 1441792 | tf_op jit(solution)/shard_map/ring_attention_backward/pallas_call | solution.py:356
  41.7 1.7 %hand_over.1 = (bf16[256,512]{1,0:T(8,128)(2,1)}, bf16[256,128]{1,0:T(8,128)(2,1)}, bf16[256,128]{1,0:T(8,128)(2,1)}) custom-call(bf16[256,512]{1,0:T(8,128)(2,1)} %get-tuple-element.6.refs_0_, bf16[256,128]{1,0:T(8,128)(2,1)} %get-tuple-element.7.refs_1_, bf16[256,128]{1,0:T(8,128)(2,1)} %get-tuple-element.8.refs_2_), custom_call_target="tpu_custom_call" | custom-call | tf_op jit(solution)/shard_map/hand_over/pallas_call | solution.py:408
